TPU v7x, 512 devices: a whole 4x4x16 slice. The times are simulated.
512 devices in a mesh: section: 8 (over x, y_lo), ctx: 64 (over y_hi, z, core).
Axes of the slice: x: 4, y: 4 (y_hi: 2, y_lo: 2; y = y_hi * 2 + y_lo), z: 16, core: 2. Of those that a mesh axis runs over, the one named last changes fastest.
Arguments:
- queries: bfloat16 [8, 8192, 3072], P('section', 'ctx'), may hold values from -6 to 6
- key_vectors: bfloat16 [8, 8192, 128], P('section', 'ctx'), may hold values from -6 to 6
- value_vectors: bfloat16 [8, 8192, 128], P('section', 'ctx'), may hold values from -6 to 6
- first_values: bfloat16 [8192, 128], P(('ctx', 'section')), may hold values from -6 to 6
- grad_out: bfloat16 [8, 8192, 3072], P('section', 'ctx'), may hold values from -6 to 6
- doc_start: int32 [8192], P('ctx'), may hold values from 0 to 8191, as said below
- mix_table: float32 [48, 256], replicated, may hold values from 0.2 to 1.2
- layer_index: int32 [8], P('section'), may hold values from 0 to 47
Outputs:
- attended: bfloat16 [8, 8192, 3072], P('section', 'ctx')
- query_grad: bfloat16 [8, 8192, 3072], P('section', 'ctx')
- key_grad: bfloat16 [8, 8192, 128], P('section', 'ctx')
- value_grad: bfloat16 [8, 8192, 128], P('section', 'ctx')
- first_grad: float32 [8192, 128], P(('ctx', 'section'))
Inputs may be any that keep to these rules, and one draw needn't show every extreme that they name: doc_start never falls, equals t where a document begins at t and 0 at t = 0, and t - doc_start[t] < 512; some document is exactly 512 positions long, and a document begins at the last position.
All inputs are finite; a program needn't handle non-finite values.
Results may differ from a plain program's by a relative error of at most 0.012.
The roundings to bfloat16 on the way count: a program that leaves them out, or rounds other values in their place, can miss the bound.
Values may be sent and summed in bfloat16 or wider, within the bound.
A program may use at most 64 MiB of HBM per device.

v0:
```python
import math

import jax
import jax.numpy as jnp
from jax import lax
from jax.sharding import PartitionSpec as P

REACH = 4


def shifted(value, axis, steps):
    count = lax.axis_size(axis)
    leading, last = (max(0, -steps), min(count, count - steps))
    return lax.ppermute(value, axis, [(source, source + steps) for source in range(leading, last)])


def window_pass(
    query_rows,
    grad_rows,
    key_window,
    value_window,
    starts,
    query_first,
    key_first,
    score_scale,
    head_count,
):
    row_count = query_rows.shape[0]
    head_width = key_window.shape[1]
    key_count = key_window.shape[0]
    query_flat = query_rows.reshape(row_count * head_count, head_width)
    grad_flat = grad_rows.reshape(row_count * head_count, head_width)
    key_positions = key_first + jnp.arange(key_count, dtype=jnp.int32)
    query_positions = query_first + jnp.arange(row_count, dtype=jnp.int32)
    allowed = (key_positions[None, :] >= starts[:, None]) & (
        key_positions[None, :] <= query_positions[:, None]
    )
    contract_last = (((1,), (1,)), ((), ()))
    contract_first = (((0,), (0,)), ((), ()))
    scores = (
        lax.dot_general(query_flat, key_window, contract_last, preferred_element_type=jnp.float32)
        * score_scale
    )
    scores = jnp.where(
        allowed[:, None, :], scores.reshape(row_count, head_count, key_count), -jnp.inf
    )
    row_max = jnp.max(scores, axis=2, keepdims=True)
    weights = jnp.exp(scores - row_max)
    weights = weights / jnp.sum(weights, axis=2, keepdims=True)
    weights = weights.reshape(row_count * head_count, key_count)
    packed = weights.astype(jnp.bfloat16)
    context = jnp.dot(packed, value_window, preferred_element_type=jnp.float32)
    grad_weights = lax.dot_general(
        grad_flat, value_window, contract_last, preferred_element_type=jnp.float32
    )
    row_dot = jnp.sum(grad_flat.astype(jnp.float32) * context, axis=1, keepdims=True)
    grad_scores = (weights * (grad_weights - row_dot)).astype(jnp.bfloat16)
    query_grad = (
        score_scale * jnp.dot(grad_scores, key_window, preferred_element_type=jnp.float32)
    ).astype(jnp.bfloat16)
    key_part = score_scale * lax.dot_general(
        grad_scores, query_flat, contract_first, preferred_element_type=jnp.float32
    )
    value_part = lax.dot_general(
        packed, grad_flat, contract_first, preferred_element_type=jnp.float32
    )
    attended = context.astype(jnp.bfloat16).reshape(row_count, head_count * head_width)
    return (attended, query_grad.reshape(row_count, head_count * head_width), key_part, value_part)


def per_device(
    queries, key_vectors, value_vectors, first_values, grad_out, doc_start, mix_table, layer_index
):
    row_count = key_vectors.shape[1]
    head_width = key_vectors.shape[2]
    head_count = queries.shape[2] // head_width
    score_scale = 1.0 / math.sqrt(head_width)
    coeffs = lax.dynamic_slice_in_dim(mix_table, layer_index[0], 1, 0)[0]
    own_coef = coeffs[:head_width]
    first_coef = coeffs[head_width:]
    first_rows = lax.all_gather(first_values, "section", axis=0, tiled=True)
    own_keys = key_vectors[0]
    mixed_values = (
        own_coef * value_vectors[0].astype(jnp.float32)
        + first_coef * first_rows.astype(jnp.float32)
    ).astype(jnp.bfloat16)
    fetched = []
    carried = (own_keys, mixed_values)
    for offset in range(REACH):
        carried = shifted((carried[0], carried[1]), "ctx", 1)
        fetched.append(carried)
    key_window = jnp.concatenate(
        [fetched[REACH - 1 - offset][0] for offset in range(REACH)] + [own_keys], axis=0
    )
    value_window = jnp.concatenate(
        [fetched[REACH - 1 - offset][1] for offset in range(REACH)] + [mixed_values], axis=0
    )
    key_count = key_window.shape[0]
    cycle_index = lax.axis_index("ctx")
    query_first = cycle_index * row_count
    key_first = query_first - REACH * row_count
    block_rows = 32
    block_count = row_count // block_rows
    section_queries = queries[0]
    section_grads = grad_out[0]

    def advance(running, block_index):
        key_sums, value_sums = running
        block_start = block_index * block_rows
        attended, query_grad, key_part, value_part = window_pass(
            lax.dynamic_slice_in_dim(section_queries, block_start, block_rows, 0),
            lax.dynamic_slice_in_dim(section_grads, block_start, block_rows, 0),
            key_window,
            value_window,
            lax.dynamic_slice_in_dim(doc_start, block_start, block_rows, 0),
            query_first + block_start,
            key_first,
            score_scale,
            head_count,
        )
        return ((key_sums + key_part, value_sums + value_part), (attended, query_grad))

    zero_sums = jnp.zeros((key_count, head_width), jnp.float32)
    (key_sums, value_sums), (attended, query_grad) = lax.scan(
        advance, (zero_sums, zero_sums), jnp.arange(block_count, dtype=jnp.int32)
    )
    partial_sums = jnp.concatenate([key_sums, value_sums], axis=1)
    pieces = [
        partial_sums[(REACH - offset) * row_count : (REACH - offset + 1) * row_count]
        for offset in range(REACH + 1)
    ]
    returned = pieces[REACH]
    for offset in reversed(range(REACH)):
        returned = shifted(returned, "ctx", -1) + pieces[offset]
    mixed_grad = returned[:, head_width:]
    key_grad = returned[:, :head_width].astype(jnp.bfloat16)[None]
    value_grad = (own_coef * mixed_grad).astype(jnp.bfloat16)[None]
    first_grad = lax.psum_scatter(
        first_coef * mixed_grad, "section", scatter_dimension=0, tiled=True
    )
    attended = attended.reshape(row_count, head_count * head_width)[None]
    query_grad = query_grad.reshape(row_count, head_count * head_width)[None]
    return (attended, query_grad, key_grad, value_grad, first_grad)


def solution(mesh):
    return jax.shard_map(
        per_device,
        mesh=mesh,
        in_specs=(
            P("section", "ctx", None),
            P("section", "ctx", None),
            P("section", "ctx", None),
            P(("ctx", "section"), None),
            P("section", "ctx", None),
            P("ctx"),
            P(),
            P("section"),
        ),
        out_specs=(
            P("section", "ctx", None),
            P("section", "ctx", None),
            P("section", "ctx", None),
            P("section", "ctx", None),
            P(("ctx", "section"), None),
        ),
        check_vma=False,
    )
```

profile of v0, /device:TPU:16, one launch (start us, length us, event | category | flops | bytes accessed | tf_op | source)
XLA Modules:
  0.0 193.6 jit_solution(13650390365815208207)
XLA Ops:
  7.2 1.9 collective-permute-start
  9.8 28.3 %all_gather.3 = bf16[128,128]{1,0:T(8,128)(2,1)S(1)} all-gather(bf16[16,128]{1,0:T(8,128)(2,1)} %param.13), channel_id=1, replica_groups=mesh['section'=8,'ctx'=64] {'section'}, dimensions={0}, use_global_device_ids=true | all-gather | bytes 36864 | tf_op jit(solution)/shard_map/all_gather | solution.py:81
  39.6 1.9 collective-permute-start.4
  41.6 3.9 %collective-permute-start.1 = (bf16[128,128]{1,0:T(8,128)(2,1)S(1)}, bf16[128,128]{1,0:T(8,128)(2,1)S(1)}, u32[]{:S(2)}, u32[]{:S(2)}) collective-permute-start(bf16[128,128]{1,0:T(8,128)(2,1)S(1)} %collective-permute-done), channel_id=1, source_target_pairs={{0,1},{1,2},{2,3},{3,4},{4,5},{5,6},{6,7},{7,8},{8,9},{9,10},{10,1... | collective-permute-start | bytes 98312 | tf_op jit(solution)/shard_map/ppermute | solution.py:14
  45.5 3.0 %collective-permute-done.4 = bf16[128,128]{1,0:T(8,128)(2,1)S(1)} collective-permute-done((bf16[128,128]{1,0:T(8,128)(2,1)S(1)}, bf16[128,128]{1,0:T(8,128)(2,1)S(1)}, u32[]{:S(2)}, u32[]{:S(2)}) %collective-permute-start.4) | collective-permute-done | bytes 32800 | tf_op jit(solution)/shard_map/ppermute | solution.py:14
  48.5 1.9 collective-permute-start.5
  50.4 1.9 collective-permute-start.2
  52.3 5.0 %collective-permute-done.5 = bf16[128,128]{1,0:T(8,128)(2,1)S(1)} collective-permute-done((bf16[128,128]{1,0:T(8,128)(2,1)S(1)}, bf16[128,128]{1,0:T(8,128)(2,1)S(1)}, u32[]{:S(2)}, u32[]{:S(2)}) %collective-permute-start.5) | collective-permute-done | bytes 32800 | tf_op jit(solution)/shard_map/ppermute | solution.py:14
  57.3 1.9 collective-permute-start.6
  59.2 1.9 collective-permute-start.3
  61.2 4.9 %collective-permute-done.6 = bf16[128,128]{1,0:T(8,128)(2,1)S(1)} collective-permute-done((bf16[128,128]{1,0:T(8,128)(2,1)S(1)}, bf16[128,128]{1,0:T(8,128)(2,1)S(1)}, u32[]{:S(2)}, u32[]{:S(2)}) %collective-permute-start.6) | collective-permute-done | bytes 32800 | tf_op jit(solution)/shard_map/ppermute | solution.py:14
  66.1 1.9 collective-permute-start.7
  68.9 6.1 %collective-permute-done.7 = bf16[128,128]{1,0:T(8,128)(2,1)S(1)} collective-permute-done((bf16[128,128]{1,0:T(8,128)(2,1)S(1)}, bf16[128,128]{1,0:T(8,128)(2,1)S(1)}, u32[]{:S(2)}, u32[]{:S(2)}) %collective-permute-start.7) | collective-permute-done | bytes 32800 | tf_op jit(solution)/shard_map/ppermute | solution.py:14
  75.0 39.0 %while.17 = (s32[]{:T(128)}, f32[640,128]{1,0:T(8,128)S(1)}, f32[640,128]{1,0:T(8,128)S(1)}, bf16[4,32,3072]{2,1,0:T(8,128)(2,1)}, bf16[4,32,3072]{2,1,0:T(8,128...) while((s32[]{:T(128)}, f32[640,128]{1,0:T(8,128)S(1)}, ...), condition=%wide.region_4.5_spmd.clone, body=%wide.region_0.4_spmd.clone.sunk | while | flops 762423680 | bytes 23077772 | solution.py:124
  77.2 0.9 constant_dynamic-slice_fusion.4
  114.2 1.9 collective-permute-start.8
  116.1 2.5 %collective-permute-done.8 = f32[128,256]{1,0:T(8,128)S(1)} collective-permute-done((f32[128,256]{1,0:T(8,128)S(1)}, f32[128,256]{1,0:T(8,128)S(1)}, u32[]{:S(2)}, u32[]{:S(2)}) %collective-permute-start.8) | collective-permute-done | bytes 131104 | tf_op jit(solution)/shard_map/ppermute | solution.py:14
  118.6 7.4 %collective-permute-start.9 = (f32[128,256]{1,0:T(8,128)S(1)}, f32[128,256]{1,0:T(8,128)S(1)}, u32[]{:S(2)}, u32[]{:S(2)}) collective-permute-start(f32[128,256]{1,0:T(8,128)S(1)} %slice_add_fusion.3), channel_id=1, source_target_pairs={{1,0},{2,1},{3,2},{4,3},{5,4},{6,5},{7,6},{8,7},{9,8},{10,9},{11,1... | collective-permute-start | bytes 393224 | tf_op jit(solution)/shard_map/ppermute | solution.py:14
  126.0 2.5 %collective-permute-done.9 = f32[128,256]{1,0:T(8,128)S(1)} collective-permute-done((f32[128,256]{1,0:T(8,128)S(1)}, f32[128,256]{1,0:T(8,128)S(1)}, u32[]{:S(2)}, u32[]{:S(2)}) %collective-permute-start.9) | collective-permute-done | bytes 131104 | tf_op jit(solution)/shard_map/ppermute | solution.py:14
  128.5 7.4 %collective-permute-start.10 = (f32[128,256]{1,0:T(8,128)S(1)}, f32[128,256]{1,0:T(8,128)S(1)}, u32[]{:S(2)}, u32[]{:S(2)}) collective-permute-start(f32[128,256]{1,0:T(8,128)S(1)} %slice_add_fusion.2), channel_id=1, source_target_pairs={{1,0},{2,1},{3,2},{4,3},{5,4},{6,5},{7,6},{8,7},{9,8},{10,9},{11,1... | collective-permute-start | bytes 393224 | tf_op jit(solution)/shard_map/ppermute | solution.py:14
  135.9 2.5 %collective-permute-done.10 = f32[128,256]{1,0:T(8,128)S(1)} collective-permute-done((f32[128,256]{1,0:T(8,128)S(1)}, f32[128,256]{1,0:T(8,128)S(1)}, u32[]{:S(2)}, u32[]{:S(2)}) %collective-permute-start.10) | collective-permute-done | bytes 131104 | tf_op jit(solution)/shard_map/ppermute | solution.py:14
  138.4 7.4 %collective-permute-start.11 = (f32[128,256]{1,0:T(8,128)S(1)}, f32[128,256]{1,0:T(8,128)S(1)}, u32[]{:S(2)}, u32[]{:S(2)}) collective-permute-start(f32[128,256]{1,0:T(8,128)S(1)} %slice_add_fusion.1), channel_id=1, source_target_pairs={{1,0},{2,1},{3,2},{4,3},{5,4},{6,5},{7,6},{8,7},{9,8},{10,9},{11,1... | collective-permute-start | bytes 393224 | tf_op jit(solution)/shard_map/ppermute | solution.py:14
  145.8 2.5 %collective-permute-done.11 = f32[128,256]{1,0:T(8,128)S(1)} collective-permute-done((f32[128,256]{1,0:T(8,128)S(1)}, f32[128,256]{1,0:T(8,128)S(1)}, u32[]{:S(2)}, u32[]{:S(2)}) %collective-permute-start.11) | collective-permute-done | bytes 131104 | tf_op jit(solution)/shard_map/ppermute | solution.py:14
  149.7 37.1 %reduce-scatter.2.cloned.1.call-done = f32[16,128]{1,0:T(8,128)} async-done(((f32[128,128]{1,0:T(8,128)}), f32[16,128]{1,0:T(8,128)}) %reduce-scatter.2.cloned.1.call-update) | async-done | bytes 8208 | tf_op jit(solution)/shard_map/reduce_scatter | solution.py:138
  (127 shorter events, 38.9 us)
Async XLA Ops:
  7.2 179.6 %reduce-scatter.2.cloned.1.call-start = ((), (), s32[]{:S(2)}) async-start(), calls=%async_computation.1 | async-start | bytes 73728 | tf_op jit(solution)/shard_map/reduce_scatter | solution.py:138
  7.2 34.3 %collective-permute-start = (bf16[128,128]{1,0:T(8,128)(2,1)}, bf16[128,128]{1,0:T(8,128)(2,1)S(1)}, u32[]{:S(2)}, u32[]{:S(2)}) collective-permute-start(bf16[128,128]{1,0:T(8,128)(2,1)} %bitcast.66), channel_id=1, source_target_pairs={{0,1},{1,2},{2,3},{3,4},{4,5},{5,6},{6,7},{7,8},{8,9},{9,10},{10,1... | collective-permute-start | bytes 98312 | tf_op jit(solution)/shard_map/ppermute | solution.py:14
  39.6 8.8 %collective-permute-start.4 = (bf16[128,128]{1,0:T(8,128)(2,1)S(1)}, bf16[128,128]{1,0:T(8,128)(2,1)S(1)}, u32[]{:S(2)}, u32[]{:S(2)}) collective-permute-start(bf16[128,128]{1,0:T(8,128)(2,1)S(1)} %fusion.6), channel_id=1, source_target_pairs={{0,1},{1,2},{2,3},{3,4},{4,5},{5,6},{6,7},{7,8},{8,9},{9,10},{10,1... | collective-permute-start | bytes 98312 | tf_op jit(solution)/shard_map/ppermute | solution.py:14
  41.6 8.8 %collective-permute-start.1 = (bf16[128,128]{1,0:T(8,128)(2,1)S(1)}, bf16[128,128]{1,0:T(8,128)(2,1)S(1)}, u32[]{:S(2)}, u32[]{:S(2)}) collective-permute-start(bf16[128,128]{1,0:T(8,128)(2,1)S(1)} %collective-permute-done), channel_id=1, source_target_pairs={{0,1},{1,2},{2,3},{3,4},{4,5},{5,6},{6,7},{7,8},{8,9},{9,10},{10,1... | collective-permute-start | bytes 98312 | tf_op jit(solution)/shard_map/ppermute | solution.py:14
  48.5 8.8 %collective-permute-start.5 = (bf16[128,128]{1,0:T(8,128)(2,1)S(1)}, bf16[128,128]{1,0:T(8,128)(2,1)S(1)}, u32[]{:S(2)}, u32[]{:S(2)}) collective-permute-start(bf16[128,128]{1,0:T(8,128)(2,1)S(1)} %collective-permute-done.4), channel_id=1, source_target_pairs={{0,1},{1,2},{2,3},{3,4},{4,5},{5,6},{6,7},{7,8},{8,9},{9,10},{10,1... | collective-permute-start | bytes 98312 | tf_op jit(solution)/shard_map/ppermute | solution.py:14
  50.4 8.8 %collective-permute-start.2 = (bf16[128,128]{1,0:T(8,128)(2,1)S(1)}, bf16[128,128]{1,0:T(8,128)(2,1)S(1)}, u32[]{:S(2)}, u32[]{:S(2)}) collective-permute-start(bf16[128,128]{1,0:T(8,128)(2,1)S(1)} %collective-permute-done.1), channel_id=1, source_target_pairs={{0,1},{1,2},{2,3},{3,4},{4,5},{5,6},{6,7},{7,8},{8,9},{9,10},{10,1... | collective-permute-start | bytes 98312 | tf_op jit(solution)/shard_map/ppermute | solution.py:14
  57.3 8.8 %collective-permute-start.6 = (bf16[128,128]{1,0:T(8,128)(2,1)S(1)}, bf16[128,128]{1,0:T(8,128)(2,1)S(1)}, u32[]{:S(2)}, u32[]{:S(2)}) collective-permute-start(bf16[128,128]{1,0:T(8,128)(2,1)S(1)} %collective-permute-done.5), channel_id=1, source_target_pairs={{0,1},{1,2},{2,3},{3,4},{4,5},{5,6},{6,7},{7,8},{8,9},{9,10},{10,1... | collective-permute-start | bytes 98312 | tf_op jit(solution)/shard_map/ppermute | solution.py:14
  59.2 8.8 %collective-permute-start.3 = (bf16[128,128]{1,0:T(8,128)(2,1)S(1)}, bf16[128,128]{1,0:T(8,128)(2,1)S(1)}, u32[]{:S(2)}, u32[]{:S(2)}) collective-permute-start(bf16[128,128]{1,0:T(8,128)(2,1)S(1)} %collective-permute-done.2), channel_id=1, source_target_pairs={{0,1},{1,2},{2,3},{3,4},{4,5},{5,6},{6,7},{7,8},{8,9},{9,10},{10,1... | collective-permute-start | bytes 98312 | tf_op jit(solution)/shard_map/ppermute | solution.py:14
  66.1 8.8 %collective-permute-start.7 = (bf16[128,128]{1,0:T(8,128)(2,1)S(1)}, bf16[128,128]{1,0:T(8,128)(2,1)S(1)}, u32[]{:S(2)}, u32[]{:S(2)}) collective-permute-start(bf16[128,128]{1,0:T(8,128)(2,1)S(1)} %collective-permute-done.6), channel_id=1, source_target_pairs={{0,1},{1,2},{2,3},{3,4},{4,5},{5,6},{6,7},{7,8},{8,9},{9,10},{10,1... | collective-permute-start | bytes 98312 | tf_op jit(solution)/shard_map/ppermute | solution.py:14
  114.2 4.4 %collective-permute-start.8 = (f32[128,256]{1,0:T(8,128)S(1)}, f32[128,256]{1,0:T(8,128)S(1)}, u32[]{:S(2)}, u32[]{:S(2)}) collective-permute-start(f32[128,256]{1,0:T(8,128)S(1)} %slice.39), channel_id=1, source_target_pairs={{1,0},{2,1},{3,2},{4,3},{5,4},{6,5},{7,6},{8,7},{9,8},{10,9},{11,1... | collective-permute-start | bytes 393224 | tf_op jit(solution)/shard_map/ppermute | solution.py:14
  118.6 9.9 %collective-permute-start.9 = (f32[128,256]{1,0:T(8,128)S(1)}, f32[128,256]{1,0:T(8,128)S(1)}, u32[]{:S(2)}, u32[]{:S(2)}) collective-permute-start(f32[128,256]{1,0:T(8,128)S(1)} %slice_add_fusion.3), channel_id=1, source_target_pairs={{1,0},{2,1},{3,2},{4,3},{5,4},{6,5},{7,6},{8,7},{9,8},{10,9},{11,1... | collective-permute-start | bytes 393224 | tf_op jit(solution)/shard_map/ppermute | solution.py:14
  128.5 9.9 %collective-permute-start.10 = (f32[128,256]{1,0:T(8,128)S(1)}, f32[128,256]{1,0:T(8,128)S(1)}, u32[]{:S(2)}, u32[]{:S(2)}) collective-permute-start(f32[128,256]{1,0:T(8,128)S(1)} %slice_add_fusion.2), channel_id=1, source_target_pairs={{1,0},{2,1},{3,2},{4,3},{5,4},{6,5},{7,6},{8,7},{9,8},{10,9},{11,1... | collective-permute-start | bytes 393224 | tf_op jit(solution)/shard_map/ppermute | solution.py:14
  138.4 9.9 %collective-permute-start.11 = (f32[128,256]{1,0:T(8,128)S(1)}, f32[128,256]{1,0:T(8,128)S(1)}, u32[]{:S(2)}, u32[]{:S(2)}) collective-permute-start(f32[128,256]{1,0:T(8,128)S(1)} %slice_add_fusion.1), channel_id=1, source_target_pairs={{1,0},{2,1},{3,2},{4,3},{5,4},{6,5},{7,6},{8,7},{9,8},{10,9},{11,1... | collective-permute-start | bytes 393224 | tf_op jit(solution)/shard_map/ppermute | solution.py:14
Sparse Core Ops, SparseCore 0:
  149.2 37.5 reduce-scatter.1
where the time goes:
time: 195 us; the launch traced here: 194 us
  waiting for transfers between devices  66.1 us (34%)
  starting transfers between devices  41.5 us (21%)
  blocking collectives  28.3 us (15%)
  local copies, waits for them, and re-layouts  24 us (12%)
  between operations  14.9 us (8%)
  matrix products  11.4 us (6%)
  other arithmetic  4.37 us (2%)
  loops' own time  3.07 us (2%)
    ppermute x12, starting transfers between devices, shifted(): lax.ppermute(value, axis, [(source, source + steps) for source in range(l...  41.4 us
    reduce_scatter x1, waiting for transfers between devices, per_device(): lax.psum_scatter(first_coef * mixed_grad, 'section', scatter_dimension=0,...  37.1 us
    ppermute x12, waiting for transfers between devices, shifted(): lax.ppermute(value, axis, [(source, source + steps) for source in range(l...  29 us
    all_gather x1, blocking collectives, per_device(): first_rows = lax.all_gather(first_values, 'section', axis=0, tiled=True)  28.3 us
  transfers between devices with their start and end apart: 13, of which 9 were waited for; matrix products, arithmetic and copies ran while one was open for 2% of the time, Pallas kernels for 0%

commit v1 on v0

v1 whole, which is shorter than its diff:
```python
import functools
import math

import jax
import jax.numpy as jnp
from jax import lax
from jax.experimental import pallas as pl
from jax.experimental.pallas import tpu as pltpu
from jax.sharding import PartitionSpec as P

REACH = 4
BF16 = jnp.bfloat16
F32 = jnp.float32
NN = (((1,), (0,)), ((), ()))
NT = (((1,), (1,)), ((), ()))
TN = (((0,), (0,)), ((), ()))


def dot(a, b, dims=NN):
    return lax.dot_general(a, b, dims, preferred_element_type=F32)


def kernel(
    n_sec, n_ctx, rows, width, heads,
    q_hbm, k_hbm, v_hbm, f_hbm, g_hbm, start_ref, mix_ref, layer_ref,
    att_hbm, dq_hbm, kg_ref, vg_ref, fg_ref,
    q, g, att, dq, kwin, vwin, vals, firsts, packed, dscores, bias,
    vparts, kparts, vsend, ksend, vrecv, krecv, eterm, erecv,
    loc, ksem, vsem, fsem, dvsem, dksem, esem,
):
    reach = REACH
    me_s = lax.axis_index("section")
    me_c = lax.axis_index("ctx")
    scale = 1.0 / math.sqrt(width)
    own = pl.ds(reach * rows, rows)
    share = rows // n_sec

    def block(j):
        return pl.ds(j * rows, rows)

    def head(h):
        return pl.ds(h * width, width)

    def sec(r):
        return lax.rem(me_s + r, n_sec)

    def ctx(o):
        return lax.rem(me_c + o + n_ctx, n_ctx)

    in_k = pltpu.make_async_copy(k_hbm, kwin.at[own], loc.at[0])
    in_f = pltpu.make_async_copy(f_hbm, firsts.at[pl.ds(me_s * share, share)], loc.at[1])
    in_v = pltpu.make_async_copy(v_hbm, vals, loc.at[2])
    in_q = pltpu.make_async_copy(q_hbm, q, loc.at[3])
    in_g = pltpu.make_async_copy(g_hbm, g, loc.at[4])
    for c in (in_k, in_f, in_v, in_q, in_g):
        c.start()

    barrier = pltpu.get_barrier_semaphore()
    for o in range(1, reach + 1):
        for sign in (1, -1):
            pl.semaphore_signal(barrier, inc=1, device_id={"section": me_s, "ctx": ctx(sign * o)})
    for r in range(1, n_sec):
        pl.semaphore_signal(barrier, inc=1, device_id={"section": sec(r), "ctx": me_c})

    starts = start_ref[...]
    keys = (me_c - reach) * rows + lax.broadcasted_iota(jnp.int32, ((reach + 1) * rows, rows), 0)
    queries = me_c * rows + lax.broadcasted_iota(jnp.int32, ((reach + 1) * rows, rows), 1)
    turned = jnp.where((keys >= starts) & (keys <= queries), 0.0, -jnp.inf).astype(F32)
    for j in range(reach + 1):
        bias[:, block(j)] = turned[j * rows : (j + 1) * rows].T

    coeffs = mix_ref[pl.ds(layer_ref[0], 1), :]
    own_coef = coeffs[:, :width]
    first_coef = coeffs[:, width:]

    in_k.wait()
    in_f.wait()
    pl.semaphore_wait(barrier, 2 * reach + n_sec - 1)

    k_out = [
        pltpu.make_async_remote_copy(
            kwin.at[own], kwin.at[block(reach - o)], ksem.at[0, o], ksem.at[1, o],
            device_id={"section": me_s, "ctx": ctx(o)})
        for o in range(1, reach + 1)
    ]
    f_out = [
        pltpu.make_async_remote_copy(
            firsts.at[pl.ds(me_s * share, share)], firsts.at[pl.ds(me_s * share, share)],
            fsem.at[0, r], fsem.at[1, r],
            device_id={"section": sec(r), "ctx": me_c})
        for r in range(1, n_sec)
    ]
    v_out = [
        pltpu.make_async_remote_copy(
            vwin.at[own], vwin.at[block(reach - o)], vsem.at[0, o], vsem.at[1, o],
            device_id={"section": me_s, "ctx": ctx(o)})
        for o in range(1, reach + 1)
    ]
    dv_out = [
        pltpu.make_async_remote_copy(
            vsend.at[block(reach - o)], vrecv.at[o - 1], dvsem.at[0, o], dvsem.at[1, o],
            device_id={"section": me_s, "ctx": ctx(-o)})
        for o in range(1, reach + 1)
    ]
    dk_out = [
        pltpu.make_async_remote_copy(
            ksend.at[block(reach - o)], krecv.at[o - 1], dksem.at[0, o], dksem.at[1, o],
            device_id={"section": me_s, "ctx": ctx(-o)})
        for o in range(1, reach + 1)
    ]
    e_out = [
        pltpu.make_async_remote_copy(
            eterm.at[pl.ds(sec(r) * share, share)], erecv.at[r], esem.at[0, r], esem.at[1, r],
            device_id={"section": sec(r), "ctx": me_c})
        for r in range(1, n_sec)
    ]
    for c in f_out:
        c.start()
    for c in k_out:
        c.start()

    in_v.wait()
    for c in f_out:
        c.wait_recv()
    vwin[own, :] = (own_coef * vals[...].astype(F32) + first_coef * firsts[...].astype(F32)).astype(BF16)
    for c in v_out:
        c.start()

    in_q.wait()
    for c in k_out:
        c.wait_recv()
    for h in range(heads):
        s = dot(q[:, head(h)], kwin[...], NT) + bias[...]
        top = jnp.max(s, axis=1, keepdims=True)
        e = jnp.exp((s - top) * scale)
        total = jnp.sum(e, axis=1, keepdims=True)
        packed[h] = (e * (1.0 / total)).astype(BF16)

    in_g.wait()
    vparts[...] = dot(
        jnp.concatenate([g[:, head(h)] for h in range(heads)], axis=0),
        packed[...].reshape(heads * rows, (reach + 1) * rows), TN)
    for j in range(reach):
        vsend[block(j), :] = vparts[:, block(j)].T.astype(BF16)
    for c in reversed(dv_out):
        c.start()

    for c in v_out:
        c.wait_recv()
    for h in range(heads):
        p = packed[h]
        c = dot(p, vwin[...])
        att[:, head(h)] = c.astype(BF16)
        gh = g[:, head(h)]
        row_dot = jnp.sum(gh.astype(F32) * c, axis=1, keepdims=True)
        dp = dot(gh, vwin[...], NT)
        dscores[h] = (p.astype(F32) * (dp - row_dot)).astype(BF16)
    out_att = pltpu.make_async_copy(att, att_hbm, loc.at[5])
    out_att.start()

    kparts[...] = scale * dot(
        jnp.concatenate([q[:, head(h)] for h in range(heads)], axis=0),
        dscores[...].reshape(heads * rows, (reach + 1) * rows), TN)
    for j in range(reach):
        ksend[block(j), :] = kparts[:, block(j)].T.astype(BF16)
    for c in reversed(dk_out):
        c.start()

    mixed_grad = vparts[:, own].T
    for c in dv_out:
        c.wait_recv()
    for o in range(reach):
        mixed_grad = mixed_grad + vrecv[o].astype(F32)
    vg_ref[...] = (own_coef * mixed_grad).astype(BF16)
    eterm[...] = first_coef * mixed_grad
    for c in e_out:
        c.start()

    for h in range(heads):
        dq[:, head(h)] = (scale * dot(dscores[h], kwin[...])).astype(BF16)
    out_dq = pltpu.make_async_copy(dq, dq_hbm, loc.at[6])
    out_dq.start()

    key_grad = kparts[:, own].T
    for c in dk_out:
        c.wait_recv()
    for o in range(reach):
        key_grad = key_grad + krecv[o].astype(F32)
    kg_ref[...] = key_grad.astype(BF16)

    for c in e_out:
        c.wait_recv()
    first_grad = eterm[pl.ds(me_s * share, share), :]
    for r in range(1, n_sec):
        first_grad = first_grad + erecv[r]
    fg_ref[...] = first_grad

    for c in k_out + f_out + v_out + dv_out + dk_out + e_out:
        c.wait_send()
    out_att.wait()
    out_dq.wait()


def solution(mesh):
    n_sec, n_ctx = mesh.shape["section"], mesh.shape["ctx"]

    def per_device(queries, keys, values, firsts, grads, starts, mix_table, layer_index):
        rows, width = keys.shape[1], keys.shape[2]
        feats = queries.shape[2]
        heads = feats // width
        share = firsts.shape[0]
        window = (REACH + 1) * rows
        hbm = pl.BlockSpec(memory_space=pl.ANY)
        vmem = pl.BlockSpec(memory_space=pltpu.VMEM)
        smem = pl.BlockSpec(memory_space=pltpu.SMEM)
        att, dq, kg, vg, fg = pl.pallas_call(
            functools.partial(kernel, n_sec, n_ctx, rows, width, heads),
            out_shape=[
                jax.ShapeDtypeStruct((rows, feats), BF16),
                jax.ShapeDtypeStruct((rows, feats), BF16),
                jax.ShapeDtypeStruct((rows, width), BF16),
                jax.ShapeDtypeStruct((rows, width), BF16),
                jax.ShapeDtypeStruct((share, width), F32),
            ],
            in_specs=[hbm, hbm, hbm, hbm, hbm, vmem, vmem, smem],
            out_specs=[hbm, hbm, vmem, vmem, vmem],
            scratch_shapes=[
                pltpu.VMEM((rows, feats), BF16),
                pltpu.VMEM((rows, feats), BF16),
                pltpu.VMEM((rows, feats), BF16),
                pltpu.VMEM((rows, feats), BF16),
                pltpu.VMEM((window, width), BF16),
                pltpu.VMEM((window, width), BF16),
                pltpu.VMEM((rows, width), BF16),
                pltpu.VMEM((rows, width), BF16),
                pltpu.VMEM((heads, rows, window), BF16),
                pltpu.VMEM((heads, rows, window), BF16),
                pltpu.VMEM((rows, window), F32),
                pltpu.VMEM((width, window), F32),
                pltpu.VMEM((width, window), F32),
                pltpu.VMEM((REACH * rows, width), BF16),
                pltpu.VMEM((REACH * rows, width), BF16),
                pltpu.VMEM((REACH, rows, width), BF16),
                pltpu.VMEM((REACH, rows, width), BF16),
                pltpu.VMEM((rows, width), F32),
                pltpu.VMEM((n_sec, share, width), F32),
                pltpu.SemaphoreType.DMA((7,)),
                pltpu.SemaphoreType.DMA((2, REACH + 1)),
                pltpu.SemaphoreType.DMA((2, REACH + 1)),
                pltpu.SemaphoreType.DMA((2, n_sec)),
                pltpu.SemaphoreType.DMA((2, REACH + 1)),
                pltpu.SemaphoreType.DMA((2, REACH + 1)),
                pltpu.SemaphoreType.DMA((2, n_sec)),
            ],
            compiler_params=pltpu.CompilerParams(
                collective_id=0, has_side_effects=True, vmem_limit_bytes=48 << 20),
            cost_estimate=pl.CostEstimate(
                flops=12 * rows * feats * window, bytes_accessed=8 * rows * feats,
                transcendentals=rows * heads * window),
            name="attention",
        )(queries[0], keys[0], values[0], firsts, grads[0], starts.reshape(1, rows), mix_table, layer_index)
        return att[None], dq[None], kg[None], vg[None], fg

    return jax.shard_map(
        per_device,
        mesh=mesh,
        in_specs=(
            P("section", "ctx", None),
            P("section", "ctx", None),
            P("section", "ctx", None),
            P(("ctx", "section"), None),
            P("section", "ctx", None),
            P("ctx"),
            P(),
            P("section"),
        ),
        out_specs=(
            P("section", "ctx", None),
            P("section", "ctx", None),
            P("section", "ctx", None),
            P("section", "ctx", None),
            P(("ctx", "section"), None),
        ),
        check_vma=False,
    )
```

time: 195 us -> 45.8 us (0.23)
  the two profiles are of different devices: /device:TPU:16 before, /device:TPU:1 now
where the time goes in v1:
time: 45.8 us; the launch traced here: 45.3 us
  Pallas kernels  35.2 us (77%)
  local copies, waits for them, and re-layouts  8.84 us (19%)
  between operations  1.31 us (3%)
    pallas_call x1, Pallas kernels, per_device(): pl.pallas_call(functools.partial(kernel, n_sec, n_ctx, rows, width, heads...  35.2 us
    unnamed x19, local copies, waits for them, and re-layouts  8.84 us

profile of v1, /device:TPU:1, one launch (start us, length us, event | category | flops | bytes accessed | tf_op | source)
XLA Modules:
  0.0 45.3 jit_solution(14649622911778286508)
XLA Ops:
  1.3 0.0 copy-start.5
  1.3 0.0 copy-start.6
  1.3 0.7 %copy-done.5 = bf16[16,128]{1,0:T(8,128)(2,1)S(1)} copy-done((bf16[16,128]{1,0:T(8,128)(2,1)S(1)}, bf16[16,128]{1,0:T(8,128)(2,1)}, u32[]{:S(2)}) %copy-start.5) | copy-done | bytes 4120
  2.0 0.0 copy-done.6
  2.0 0.0 copy-start
  2.0 1.1 %copy-done = bf16[1,128,3072]{2,1,0:T(8,128)(2,1)S(1)} copy-done((bf16[1,128,3072]{2,1,0:T(8,128)(2,1)S(1)}, bf16[1,128,3072]{2,1,0:T(8,128)(2,1)}, u32[]{:S(2)}) %copy-start) | copy-done | bytes 786456
  3.1 0.0 copy-start.1
  3.1 1.1 %copy-done.1 = bf16[1,128,3072]{2,1,0:T(8,128)(2,1)S(1)} copy-done((bf16[1,128,3072]{2,1,0:T(8,128)(2,1)S(1)}, bf16[1,128,3072]{2,1,0:T(8,128)(2,1)}, u32[]{:S(2)}) %copy-start.1) | copy-done | bytes 786456
  4.2 0.0 copy-start.2
  4.2 0.8 %copy-done.2 = f32[48,256]{1,0:T(8,128)S(1)} copy-done((f32[48,256]{1,0:T(8,128)S(1)}, f32[48,256]{1,0:T(8,128)}, u32[]{:S(2)}) %copy-start.2) | copy-done | bytes 49176
  5.0 0.0 copy-start.3
  5.0 0.8 %copy-done.3 = bf16[1,128,128]{2,1,0:T(8,128)(2,1)S(1)} copy-done((bf16[1,128,128]{2,1,0:T(8,128)(2,1)S(1)}, bf16[1,128,128]{2,1,0:T(8,128)(2,1)}, u32[]{:S(2)}) %copy-start.3) | copy-done | bytes 32792
  5.8 0.0 copy-start.4
  5.8 0.8 %copy-done.4 = bf16[1,128,128]{2,1,0:T(8,128)(2,1)S(1)} copy-done((bf16[1,128,128]{2,1,0:T(8,128)(2,1)S(1)}, bf16[1,128,128]{2,1,0:T(8,128)(2,1)}, u32[]{:S(2)}) %copy-start.4) | copy-done | bytes 32792
  6.6 35.2 %attention.1 = (bf16[128,3072]{1,0:T(8,128)(2,1)S(1)}, bf16[128,3072]{1,0:T(8,128)(2,1)S(1)}, bf16[128,128]{1,0:T(8,128)(2,1)S(1)}, bf16[128,128]{1,0:T(8,128)(2,1)S(1)}, f32[16,128]{1,0:T(8,128)S(1)}) custom-call(bf16[128,3072]{1,0:T(8,128)(2,1)S(1)} %bitcast.13, bf16[128,128]{1,0:T(8,128)(2,1)S(1)} %bitcast.15, bf16[128,128]{1,0:T(8,128)(2,1)S(1)} %bitcast.16, ...), custom_call_target="tpu_custom_call" | custom-call | flops 3019898880 | bytes 3145728 | tf_op jit(solution)/shard_map/attention/pallas_call | solution.py:216
  41.7 0.9 %copy.19 = bf16[1,128,3072]{2,1,0:T(8,128)(2,1)} copy(bf16[1,128,3072]{2,1,0:T(8,128)(2,1)S(1)} %bitcast.10) | data formatting | bytes 1572864
  42.6 0.9 %copy.20 = bf16[1,128,3072]{2,1,0:T(8,128)(2,1)} copy(bf16[1,128,3072]{2,1,0:T(8,128)(2,1)S(1)} %bitcast.9) | data formatting | bytes 1572864
  43.5 0.6 %copy.21 = bf16[1,128,128]{2,1,0:T(8,128)(2,1)} copy(bf16[1,128,128]{2,1,0:T(8,128)(2,1)S(1)} %bitcast.12) | data formatting | bytes 65536
  44.1 0.6 %copy.22 = bf16[1,128,128]{2,1,0:T(8,128)(2,1)} copy(bf16[1,128,128]{2,1,0:T(8,128)(2,1)S(1)} %bitcast.11) | data formatting | bytes 65536
  44.7 0.6 %copy.23 = f32[16,128]{1,0:T(8,128)} copy(f32[16,128]{1,0:T(8,128)S(1)} %get-tuple-element.24) | data formatting | bytes 16384
Async XLA Ops:
  1.3 0.7 %copy-start.5 = (bf16[16,128]{1,0:T(8,128)(2,1)S(1)}, bf16[16,128]{1,0:T(8,128)(2,1)}, u32[]{:S(2)}) copy-start(bf16[16,128]{1,0:T(8,128)(2,1)} %f_hbm.1) | copy-start | bytes 12292
  1.3 0.7 %copy-start.6 = (s32[128]{0:T(128)S(1)}, s32[128]{0:T(128)}, u32[]{:S(2)}) copy-start(s32[128]{0:T(128)} %param.13) | copy-start | bytes 1540
  2.0 1.1 %copy-start = (bf16[1,128,3072]{2,1,0:T(8,128)(2,1)S(1)}, bf16[1,128,3072]{2,1,0:T(8,128)(2,1)}, u32[]{:S(2)}) copy-start(bf16[1,128,3072]{2,1,0:T(8,128)(2,1)} %param.8) | copy-start | bytes 2359300
  3.1 1.1 %copy-start.1 = (bf16[1,128,3072]{2,1,0:T(8,128)(2,1)S(1)}, bf16[1,128,3072]{2,1,0:T(8,128)(2,1)}, u32[]{:S(2)}) copy-start(bf16[1,128,3072]{2,1,0:T(8,128)(2,1)} %param.12) | copy-start | bytes 2359300
  4.2 0.8 %copy-start.2 = (f32[48,256]{1,0:T(8,128)S(1)}, f32[48,256]{1,0:T(8,128)}, u32[]{:S(2)}) copy-start(f32[48,256]{1,0:T(8,128)} %mix_ref.1) | copy-start | bytes 147460
  5.0 0.8 %copy-start.3 = (bf16[1,128,128]{2,1,0:T(8,128)(2,1)S(1)}, bf16[1,128,128]{2,1,0:T(8,128)(2,1)}, u32[]{:S(2)}) copy-start(bf16[1,128,128]{2,1,0:T(8,128)(2,1)} %param.9) | copy-start | bytes 98308
  5.8 0.8 %copy-start.4 = (bf16[1,128,128]{2,1,0:T(8,128)(2,1)S(1)}, bf16[1,128,128]{2,1,0:T(8,128)(2,1)}, u32[]{:S(2)}) copy-start(bf16[1,128,128]{2,1,0:T(8,128)(2,1)} %param.10) | copy-start | bytes 98308

commit v2 on v1

v2 whole, which is shorter than its diff:
```python
import functools
import math

import jax
import jax.numpy as jnp
from jax import lax
from jax.experimental import pallas as pl
from jax.experimental.pallas import tpu as pltpu
from jax.sharding import PartitionSpec as P

REACH = 4
BF16 = jnp.bfloat16
F32 = jnp.float32
NN = (((1,), (0,)), ((), ()))
NT = (((1,), (1,)), ((), ()))
TN = (((0,), (0,)), ((), ()))


def dot(a, b, dims=NN):
    return lax.dot_general(a, b, dims, preferred_element_type=F32)


def kernel(
    n_sec, n_ctx, rows, width, heads,
    q_hbm, k_hbm, v_hbm, f_hbm, g_hbm, start_hbm, mix_hbm, layer_ref,
    att, dq, kg, vg, fg,
    q, g, kwin, vwin, vraw, fpart, fall, starts, mix, packed, dscores, bias,
    vparts, kparts, vhome, khome, vpair, kpair, vback, kback, rsend, rrecv, rhome, rback,
    loc, ksem, vsem, fzsem, fssem, dvsem, dksem, essem, rzsem,
):
    me_s = lax.axis_index("section")
    me_c = lax.axis_index("ctx")
    odd = lax.rem(me_c, 2)
    scale = 1.0 / math.sqrt(width)
    share = rows // n_sec
    mine = (0, 2, 4)

    def block(j):
        return pl.ds(j * rows, rows)

    def part(b):
        return pl.ds(b * share, share)

    def head(h):
        return pl.ds(h * width, width)

    def at_sec(r):
        return {"section": lax.rem(me_s + r, n_sec), "ctx": me_c}

    def at_ctx(o):
        return {"section": me_s, "ctx": me_c + o}

    mate = {"section": me_s, "ctx": me_c + 1 - 2 * odd}
    own = block(REACH)
    near = pl.ds((4 - 2 * odd) * rows, rows)
    far = pl.ds((2 - 2 * odd) * rows, rows)

    def remote(src, dst, sems, i, device):
        return pltpu.make_async_remote_copy(src, dst, sems.at[0, i], sems.at[1, i], device_id=device)

    loads = [
        pltpu.make_async_copy(a, b, loc.at[i])
        for i, (a, b) in enumerate([
            (k_hbm, kwin.at[own]),
            (f_hbm, fpart.at[part(2)]),
            (v_hbm, vraw.at[own]),
            (start_hbm, starts),
            (mix_hbm, mix),
            (q_hbm, q),
            (g_hbm, g),
        ])
    ]
    in_k, in_f, in_v, in_start, in_mix, in_q, in_g = loads

    back2, back4 = me_c >= 2, me_c >= 4
    on2, on4 = me_c + 2 < n_ctx, me_c + 4 < n_ctx

    barrier = pltpu.get_barrier_semaphore()
    for there, o in ((on4, 4), (on2, 2), (back2, -2), (back4, -4)):
        @pl.when(there)
        def _():
            pl.semaphore_signal(barrier, inc=1, device_id=at_ctx(o))
    pl.semaphore_signal(barrier, inc=1, device_id=mate)
    for r in range(1, n_sec):
        pl.semaphore_signal(barrier, inc=1, device_id=at_sec(r))
    for c in loads:
        c.start()

    fz1 = remote(f_hbm, fpart.at[part(1)], fzsem, 0, at_ctx(2))
    fz2 = remote(f_hbm, fpart.at[part(0)], fzsem, 1, at_ctx(4))
    fs = [remote(fpart, fall.at[me_s], fssem, r, at_sec(r)) for r in range(1, n_sec)]
    k1 = remote(k_hbm, kwin.at[block(2)], ksem, 0, at_ctx(2))
    k2 = remote(k_hbm, kwin.at[block(0)], ksem, 1, at_ctx(4))
    k3 = remote(kwin.at[near], kwin.at[block(3)], ksem, 2, mate)
    k4 = remote(kwin.at[far], kwin.at[block(1)], ksem, 3, mate)
    v1 = remote(v_hbm, vraw.at[block(2)], vsem, 0, at_ctx(2))
    v2 = remote(v_hbm, vraw.at[block(0)], vsem, 1, at_ctx(4))
    v3 = remote(vwin.at[near], vwin.at[block(3)], vsem, 2, mate)
    v4 = remote(vwin.at[far], vwin.at[block(1)], vsem, 3, mate)
    dv1 = remote(vhome.at[block(2)], vback.at[0], dvsem, 0, at_ctx(-2))
    dv2 = remote(vhome.at[block(0)], vback.at[1], dvsem, 1, at_ctx(-4))
    dv3 = remote(vhome.at[block(3)], vpair.at[0], dvsem, 2, mate)
    dv4 = remote(vhome.at[block(1)], vpair.at[1], dvsem, 3, mate)
    dk1 = remote(khome.at[block(2)], kback.at[0], dksem, 0, at_ctx(-2))
    dk2 = remote(khome.at[block(0)], kback.at[1], dksem, 1, at_ctx(-4))
    dk3 = remote(khome.at[block(3)], kpair.at[0], dksem, 2, mate)
    dk4 = remote(khome.at[block(1)], kpair.at[1], dksem, 3, mate)
    es = [remote(rsend.at[lax.rem(me_s + r, n_sec)], rrecv.at[r], essem, r, at_sec(r)) for r in range(1, n_sec)]
    rz1 = remote(rhome.at[part(1)], rback.at[0], rzsem, 0, at_ctx(-2))
    rz2 = remote(rhome.at[part(0)], rback.at[1], rzsem, 1, at_ctx(-4))

    @pl.when(jnp.logical_not(back4))
    def _():
        for ref, size in ((kwin, rows), (vraw, rows), (fpart, share)):
            ref[pl.ds(0, size), :] = jnp.zeros((size, width), BF16)

    @pl.when(jnp.logical_not(back2))
    def _():
        for ref, lo, size in ((kwin, 2 * rows, rows), (vraw, 2 * rows, rows), (fpart, share, share)):
            ref[pl.ds(lo, size), :] = jnp.zeros((size, width), BF16)

    for there, i in ((on2, 0), (on4, 1)):
        @pl.when(jnp.logical_not(there))
        def _():
            for ref in (vback, kback, rback):
                ref[i] = jnp.zeros(ref.shape[1:], ref.dtype)

    def near_far(there2, there4, *actions):
        for act2, act4 in actions:
            pl.when(there4)(act4)
            pl.when(there2)(act2)

    ahead = lax.convert_element_type(on2, jnp.int32) + lax.convert_element_type(on4, jnp.int32)
    behind = lax.convert_element_type(back2, jnp.int32) + lax.convert_element_type(back4, jnp.int32)
    pl.semaphore_wait(barrier, n_sec + ahead + behind)
    near_far(on2, on4, (fz1.start, fz2.start), (k1.start, k2.start), (v1.start, v2.start))
    in_k.wait()

    @pl.when(odd == 0)
    def _():
        k3.start()

    in_start.wait()
    window = (REACH + 1) * rows
    key_at = (me_c - REACH) * rows + lax.broadcasted_iota(jnp.int32, (window, rows), 0)
    query_at = me_c * rows + lax.broadcasted_iota(jnp.int32, (window, rows), 1)
    turned = jnp.where((key_at >= starts[...]) & (key_at <= query_at), 0.0, -jnp.inf).astype(F32)
    for j in range(REACH + 1):
        bias[:, block(j)] = turned[j * rows : (j + 1) * rows].T

    in_mix.wait()
    coeffs = mix[pl.ds(layer_ref[0], 1), :]
    own_coef = coeffs[:, :width]
    first_coef = coeffs[:, width:]

    in_f.wait()

    @pl.when(back2)
    def _():
        k1.wait_recv()

    @pl.when(odd == 0)
    def _():
        k4.start()

    @pl.when(odd == 1)
    def _():
        k3.start()

    near_far(back2, back4, (fz1.wait_recv, fz2.wait_recv))
    for c in fs:
        c.start()
    in_q.wait()

    @pl.when(back4)
    def _():
        k2.wait_recv()

    @pl.when(odd == 1)
    def _():
        k4.start()

    k3.wait_recv()
    k4.wait_recv()
    for h in range(heads):
        s = dot(q[:, head(h)], kwin[...], NT) + bias[...]
        top = jnp.max(s, axis=1, keepdims=True)
        e = jnp.exp((s - top) * scale)
        total = jnp.sum(e, axis=1, keepdims=True)
        packed[h] = (e * (1.0 / total)).astype(BF16)

    in_v.wait()
    near_far(back2, back4, (v1.wait_recv, v2.wait_recv))
    fall[me_s] = fpart[...]
    for c in fs:
        c.wait_recv()
    for b in (2, 1, 0):
        firsts = jnp.concatenate([fall[s, b * share : (b + 1) * share, :] for s in range(n_sec)], axis=0)
        vwin[block(mine[b]), :] = (
            own_coef * vraw[block(mine[b]), :].astype(F32) + first_coef * firsts.astype(F32)
        ).astype(BF16)
    v3.start()
    v4.start()

    in_g.wait()
    g_rows = jnp.concatenate([g[:, head(h)] for h in range(heads)], axis=0)
    for lo, hi in ((0, 2), (2, 4), (4, 5)):
        turned_sum = dot(g_rows, packed[:, :, lo * rows : hi * rows].reshape(heads * rows, (hi - lo) * rows), TN)
        for j in range(lo, hi):
            vparts[block(j), :] = turned_sum[:, (j - lo) * rows : (j - lo + 1) * rows].T
        if lo == 0:
            vhome[block(1), :] = vparts[block(1), :].astype(BF16)
            dv4.start()
        if lo == 2:
            vhome[block(3), :] = vparts[block(3), :].astype(BF16)
            dv3.start()
    v3.wait_recv()
    v4.wait_recv()

    for h in range(heads):
        if h == heads // 2:
            dv4.wait_recv()
            dv3.wait_recv()
            vparts[far, :] = vparts[far, :] + vpair[1].astype(F32)
            vparts[near, :] = vparts[near, :] + vpair[0].astype(F32)
            vhome[block(0), :] = vparts[block(0), :].astype(BF16)
            vhome[block(2), :] = vparts[block(2), :].astype(BF16)
            near_far(back2, back4, (dv1.start, dv2.start))
            for b in range(3):
                term = (first_coef * vparts[block(mine[b]), :]).astype(BF16)
                for s in range(n_sec):
                    rsend[s, b * share : (b + 1) * share, :] = term[s * share : (s + 1) * share]
            for c in es:
                c.start()
        p = packed[h]
        c = dot(p, vwin[...])
        att[:, head(h)] = c.astype(BF16)
        gh = g[:, head(h)]
        row_dot = jnp.sum(gh.astype(F32) * c, axis=1, keepdims=True)
        dp = dot(gh, vwin[...], NT)
        dscores[h] = (p.astype(F32) * (dp - row_dot)).astype(BF16)

    q_rows = jnp.concatenate([q[:, head(h)] for h in range(heads)], axis=0)
    for lo, hi in ((0, 2), (2, 4), (4, 5)):
        turned_sum = scale * dot(
            q_rows, dscores[:, :, lo * rows : hi * rows].reshape(heads * rows, (hi - lo) * rows), TN)
        for j in range(lo, hi):
            kparts[block(j), :] = turned_sum[:, (j - lo) * rows : (j - lo + 1) * rows].T
        if lo == 0:
            khome[block(1), :] = kparts[block(1), :].astype(BF16)
            dk4.start()
        if lo == 2:
            khome[block(3), :] = kparts[block(3), :].astype(BF16)
            dk3.start()
    dk4.wait_recv()
    dk3.wait_recv()
    kparts[far, :] = kparts[far, :] + kpair[1].astype(F32)
    kparts[near, :] = kparts[near, :] + kpair[0].astype(F32)
    khome[block(0), :] = kparts[block(0), :].astype(BF16)
    khome[block(2), :] = kparts[block(2), :].astype(BF16)
    near_far(back2, back4, (dk1.start, dk2.start))

    for c in es:
        c.wait_recv()
    total = rsend[me_s].astype(F32)
    for r in range(1, n_sec):
        total = total + rrecv[r].astype(F32)
    rhome[...] = total
    near_far(back2, back4, (rz1.start, rz2.start))

    near_far(on2, on4, (dv1.wait_recv, dv2.wait_recv))
    vg[...] = (own_coef * (vparts[own, :] + vback[0].astype(F32) + vback[1].astype(F32))).astype(BF16)

    for h in range(heads):
        dq[:, head(h)] = (scale * dot(dscores[h], kwin[...])).astype(BF16)

    near_far(on2, on4, (rz1.wait_recv, rz2.wait_recv))
    fg[...] = rhome[part(2), :] + rback[0] + rback[1]
    near_far(on2, on4, (dk1.wait_recv, dk2.wait_recv))
    kg[...] = (kparts[own, :] + kback[0].astype(F32) + kback[1].astype(F32)).astype(BF16)

    for c in fs + es + [k3, k4, v3, v4, dv3, dv4, dk3, dk4]:
        c.wait_send()
    near_far(on2, on4, *[(a.wait_send, b.wait_send) for a, b in ((fz1, fz2), (k1, k2), (v1, v2))])
    near_far(back2, back4, *[(a.wait_send, b.wait_send) for a, b in ((dv1, dv2), (dk1, dk2), (rz1, rz2))])


def place(*refs):
    n = (len(refs) - 1) // 2
    copies = [pltpu.make_async_copy(refs[i], refs[n + i], refs[-1].at[i]) for i in range(n)]
    for c in copies:
        c.start()
    for c in copies:
        c.wait()


def solution(mesh):
    n_sec, n_ctx = mesh.shape["section"], mesh.shape["ctx"]

    def per_device(queries, keys, values, firsts, grads, starts, mix_table, layer_index):
        rows, width = keys.shape[1], keys.shape[2]
        feats = queries.shape[2]
        heads = feats // width
        share = firsts.shape[0]
        window = (REACH + 1) * rows
        piece = 3 * share
        hbm = pl.BlockSpec(memory_space=pltpu.HBM)
        anyw = pl.BlockSpec(memory_space=pl.ANY)
        smem = pl.BlockSpec(memory_space=pltpu.SMEM)
        vmem = pl.BlockSpec(memory_space=pltpu.VMEM)
        shapes = [
            jax.ShapeDtypeStruct((rows, feats), BF16),
            jax.ShapeDtypeStruct((rows, feats), BF16),
            jax.ShapeDtypeStruct((rows, width), BF16),
            jax.ShapeDtypeStruct((rows, width), BF16),
            jax.ShapeDtypeStruct((share, width), F32),
        ]
        four = pltpu.SemaphoreType.DMA((2, 4))
        two = pltpu.SemaphoreType.DMA((2, 2))
        results = pl.pallas_call(
            functools.partial(kernel, n_sec, n_ctx, rows, width, heads),
            out_shape=[pltpu.VMEM(x.shape, x.dtype) for x in shapes],
            in_specs=[hbm] * 7 + [smem],
            out_specs=[vmem] * 5,
            scratch_shapes=[
                pltpu.VMEM((rows, feats), BF16),
                pltpu.VMEM((rows, feats), BF16),
                pltpu.VMEM((window, width), BF16),
                pltpu.VMEM((window, width), BF16),
                pltpu.VMEM((window, width), BF16),
                pltpu.VMEM((piece, width), BF16),
                pltpu.VMEM((n_sec, piece, width), BF16),
                pltpu.VMEM((1, rows), jnp.int32),
                pltpu.VMEM(mix_table.shape, F32),
                pltpu.VMEM((heads, rows, window), BF16),
                pltpu.VMEM((heads, rows, window), BF16),
                pltpu.VMEM((rows, window), F32),
                pltpu.VMEM((window, width), F32),
                pltpu.VMEM((window, width), F32),
                pltpu.VMEM((REACH * rows, width), BF16),
                pltpu.VMEM((REACH * rows, width), BF16),
                pltpu.VMEM((2, rows, width), BF16),
                pltpu.VMEM((2, rows, width), BF16),
                pltpu.VMEM((2, rows, width), BF16),
                pltpu.VMEM((2, rows, width), BF16),
                pltpu.VMEM((n_sec, piece, width), BF16),
                pltpu.VMEM((n_sec, piece, width), BF16),
                pltpu.VMEM((piece, width), F32),
                pltpu.VMEM((2, share, width), F32),
                pltpu.SemaphoreType.DMA((7,)),
                four,
                four,
                two,
                pltpu.SemaphoreType.DMA((2, n_sec)),
                four,
                four,
                pltpu.SemaphoreType.DMA((2, n_sec)),
                two,
            ],
            compiler_params=pltpu.CompilerParams(
                collective_id=0, has_side_effects=True, vmem_limit_bytes=48 << 20),
            cost_estimate=pl.CostEstimate(
                flops=12 * rows * feats * window, bytes_accessed=8 * rows * feats,
                transcendentals=rows * heads * window),
            name="attention",
        )(*[
            pltpu.with_memory_space_constraint(x, pltpu.HBM)
            for x in (queries[0], keys[0], values[0], firsts, grads[0], starts.reshape(1, rows), mix_table)
        ], layer_index)
        att, dq, kg, vg, fg = pl.pallas_call(
            place,
            out_shape=shapes,
            in_specs=[anyw] * 5,
            out_specs=[hbm] * 5,
            scratch_shapes=[pltpu.SemaphoreType.DMA((5,))],
            compiler_params=pltpu.CompilerParams(vmem_limit_bytes=8 << 20),
            name="place",
        )(*results)
        return att[None], dq[None], kg[None], vg[None], fg

    return jax.shard_map(
        per_device,
        mesh=mesh,
        in_specs=(
            P("section", "ctx", None),
            P("section", "ctx", None),
            P("section", "ctx", None),
            P(("ctx", "section"), None),
            P("section", "ctx", None),
            P("ctx"),
            P(),
            P("section"),
        ),
        out_specs=(
            P("section", "ctx", None),
            P("section", "ctx", None),
            P("section", "ctx", None),
            P("section", "ctx", None),
            P(("ctx", "section"), None),
        ),
        check_vma=False,
    )
```

time: 45.8 us -> 37.1 us (0.81)
  the two profiles are of different devices: /device:TPU:1 before, /device:TPU:16 now
where the time goes in v2:
time: 37.1 us; the launch traced here: 36.7 us
  Pallas kernels  35.4 us (95%)
  between operations  1.29 us (3%)
    pallas_call x1, Pallas kernels, per_device(): pl.pallas_call(functools.partial(kernel, n_sec, n_ctx, rows, width, heads...  34.2 us
    pallas_call x1, Pallas kernels, per_device(): pl.pallas_call(place, out_shape=shapes, in_specs=[anyw] * 5, out_specs=[h...  1.19 us

profile of v2, /device:TPU:16, one launch (start us, length us, event | category | flops | bytes accessed | tf_op | source)
XLA Modules:
  0.0 36.7 jit_solution(18034307872762721551)
XLA Ops:
  1.3 34.2 %attention.1 = (bf16[128,3072]{1,0:T(8,128)(2,1)S(1)}, bf16[128,3072]{1,0:T(8,128)(2,1)S(1)}, bf16[128,128]{1,0:T(8,128)(2,1)S(1)}, bf16[128,128]{1,0:T(8,128)(2,1)S(1)}, f32[16,128]{1,0:T(8,128)S(1)}) custom-call(bf16[128,3072]{1,0:T(8,128)(2,1)} %bitcast.9, bf16[128,128]{1,0:T(8,128)(2,1)} %bitcast.13, bf16[128,128]{1,0:T(8,128)(2,1)} %bitcast.14, ...), custom_call_target="tpu_custom_call" | custom-call | flops 3019898880 | bytes 3145728 | tf_op jit(solution)/shard_map/attention/pallas_call | solution.py:320
  35.5 1.2 %place.1 = (bf16[128,3072]{1,0:T(8,128)(2,1)}, bf16[128,3072]{1,0:T(8,128)(2,1)}, bf16[128,128]{1,0:T(8,128)(2,1)}, bf16[128,128]{1,0:T(8,128)(2,1)}, f32[16,128]{1,0:T(8,128)}) custom-call(bf16[128,3072]{1,0:T(8,128)(2,1)S(1)} %get-tuple-element.15.refs_0_, bf16[128,3072]{1,0:T(8,128)(2,1)S(1)} %get-tuple-element.16.refs_1_, ...), custom_call_target="tpu_custom_call" | custom-call | tf_op jit(solution)/shard_map/place/pallas_call | solution.py:370

commit v3 on v2

--- a/solution.py
+++ b/solution.py
@@ -13,7 +13,6 @@
 F32 = jnp.float32
 NN = (((1,), (0,)), ((), ()))
 NT = (((1,), (1,)), ((), ()))
-TN = (((0,), (0,)), ((), ()))
 
 
 def dot(a, b, dims=NN):
@@ -25,6 +24,7 @@
     q_hbm, k_hbm, v_hbm, f_hbm, g_hbm, start_hbm, mix_hbm, layer_ref,
     att, dq, kg, vg, fg,
     q, g, kwin, vwin, vraw, fpart, fall, starts, mix, packed, dscores, bias,
+    q_turned, g_turned, early, early_top, early_sum,
     vparts, kparts, vhome, khome, vpair, kpair, vback, kback, rsend, rrecv, rhome, rback,
     loc, ksem, vsem, fzsem, fssem, dvsem, dksem, essem, rzsem,
 ):
@@ -130,10 +130,16 @@
             pl.when(there4)(act4)
             pl.when(there2)(act2)
 
+    in_q.wait()
+    for h in range(heads):
+        q_turned[:, head(h)] = q[:, head(h)].T
+    in_g.wait()
+    for h in range(heads):
+        g_turned[:, head(h)] = g[:, head(h)].T
     ahead = lax.convert_element_type(on2, jnp.int32) + lax.convert_element_type(on4, jnp.int32)
     behind = lax.convert_element_type(back2, jnp.int32) + lax.convert_element_type(back4, jnp.int32)
     pl.semaphore_wait(barrier, n_sec + ahead + behind)
-    near_far(on2, on4, (fz1.start, fz2.start), (k1.start, k2.start), (v1.start, v2.start))
+    near_far(on2, on4, (fz1.start, fz2.start), (k1.start, k2.start))
     in_k.wait()
 
     @pl.when(odd == 0)
@@ -167,10 +173,21 @@
     def _():
         k3.start()
 
+    near_far(on2, on4, (v1.start, v2.start))
     near_far(back2, back4, (fz1.wait_recv, fz2.wait_recv))
     for c in fs:
         c.start()
-    in_q.wait()
+    for h in range(heads):
+        qh = q[:, head(h)]
+        s4 = dot(qh, kwin[block(4), :], NT) + bias[:, block(4)]
+        s2 = dot(qh, kwin[block(2), :], NT) + bias[:, block(2)]
+        top = jnp.max(jnp.maximum(s4, s2), axis=1, keepdims=True)
+        e4 = jnp.exp((s4 - top) * scale)
+        e2 = jnp.exp((s2 - top) * scale)
+        early[h, :, :rows] = e2
+        early[h, :, rows:] = e4
+        early_top[h] = jnp.broadcast_to(top, (rows, width))
+        early_sum[h] = jnp.broadcast_to(jnp.sum(e4 + e2, axis=1, keepdims=True), (rows, width))
 
     @pl.when(back4)
     def _():
@@ -183,11 +200,22 @@
     k3.wait_recv()
     k4.wait_recv()
     for h in range(heads):
-        s = dot(q[:, head(h)], kwin[...], NT) + bias[...]
-        top = jnp.max(s, axis=1, keepdims=True)
-        e = jnp.exp((s - top) * scale)
-        total = jnp.sum(e, axis=1, keepdims=True)
-        packed[h] = (e * (1.0 / total)).astype(BF16)
+        qh = q[:, head(h)]
+        s0 = dot(qh, kwin[pl.ds(0, 2 * rows), :], NT) + bias[:, : 2 * rows]
+        s3 = dot(qh, kwin[block(3), :], NT) + bias[:, block(3)]
+        late_top = jnp.max(jnp.maximum(jnp.maximum(s0[:, :rows], s0[:, rows:]), s3), axis=1, keepdims=True)
+        top = jnp.maximum(early_top[h], late_top)
+        e0 = jnp.exp((s0[:, :rows] - top) * scale)
+        e1 = jnp.exp((s0[:, rows:] - top) * scale)
+        e3 = jnp.exp((s3 - top) * scale)
+        fade = jnp.exp((early_top[h] - top) * scale)
+        inverse = 1.0 / (jnp.sum(e0 + e1 + e3, axis=1, keepdims=True) + early_sum[h] * fade)
+        fade = fade * inverse
+        packed[h, :, block(0)] = (e0 * inverse).astype(BF16)
+        packed[h, :, block(1)] = (e1 * inverse).astype(BF16)
+        packed[h, :, block(2)] = (early[h, :, :rows] * fade).astype(BF16)
+        packed[h, :, block(3)] = (e3 * inverse).astype(BF16)
+        packed[h, :, block(4)] = (early[h, :, rows:] * fade).astype(BF16)
 
     in_v.wait()
     near_far(back2, back4, (v1.wait_recv, v2.wait_recv))
@@ -202,10 +230,8 @@
     v3.start()
     v4.start()
 
-    in_g.wait()
-    g_rows = jnp.concatenate([g[:, head(h)] for h in range(heads)], axis=0)
     for lo, hi in ((0, 2), (2, 4), (4, 5)):
-        turned_sum = dot(g_rows, packed[:, :, lo * rows : hi * rows].reshape(heads * rows, (hi - lo) * rows), TN)
+        turned_sum = dot(g_turned[...], packed[:, :, lo * rows : hi * rows].reshape(heads * rows, (hi - lo) * rows))
         for j in range(lo, hi):
             vparts[block(j), :] = turned_sum[:, (j - lo) * rows : (j - lo + 1) * rows].T
         if lo == 0:
@@ -218,7 +244,7 @@
     v4.wait_recv()
 
     for h in range(heads):
-        if h == heads // 2:
+        if h == heads // 4:
             dv4.wait_recv()
             dv3.wait_recv()
             vparts[far, :] = vparts[far, :] + vpair[1].astype(F32)
@@ -240,25 +266,27 @@
         dp = dot(gh, vwin[...], NT)
         dscores[h] = (p.astype(F32) * (dp - row_dot)).astype(BF16)
 
-    q_rows = jnp.concatenate([q[:, head(h)] for h in range(heads)], axis=0)
-    for lo, hi in ((0, 2), (2, 4), (4, 5)):
+    def key_terms(lo, hi):
         turned_sum = scale * dot(
-            q_rows, dscores[:, :, lo * rows : hi * rows].reshape(heads * rows, (hi - lo) * rows), TN)
+            q_turned[...], dscores[:, :, lo * rows : hi * rows].reshape(heads * rows, (hi - lo) * rows))
         for j in range(lo, hi):
             kparts[block(j), :] = turned_sum[:, (j - lo) * rows : (j - lo + 1) * rows].T
-        if lo == 0:
-            khome[block(1), :] = kparts[block(1), :].astype(BF16)
-            dk4.start()
-        if lo == 2:
-            khome[block(3), :] = kparts[block(3), :].astype(BF16)
-            dk3.start()
+
+    key_terms(0, 2)
+    khome[block(1), :] = kparts[block(1), :].astype(BF16)
+    dk4.start()
+    key_terms(2, 4)
+    khome[block(3), :] = kparts[block(3), :].astype(BF16)
+    dk3.start()
+    key_terms(4, 5)
     dk4.wait_recv()
+    kparts[far, :] = kparts[far, :] + kpair[1].astype(F32)
+    khome[block(0), :] = kparts[block(0), :].astype(BF16)
+    pl.when(back4)(dk2.start)
     dk3.wait_recv()
-    kparts[far, :] = kparts[far, :] + kpair[1].astype(F32)
     kparts[near, :] = kparts[near, :] + kpair[0].astype(F32)
-    khome[block(0), :] = kparts[block(0), :].astype(BF16)
     khome[block(2), :] = kparts[block(2), :].astype(BF16)
-    near_far(back2, back4, (dk1.start, dk2.start))
+    pl.when(back2)(dk1.start)
 
     for c in es:
         c.wait_recv()
@@ -335,6 +363,11 @@
                 pltpu.VMEM((heads, rows, window), BF16),
                 pltpu.VMEM((heads, rows, window), BF16),
                 pltpu.VMEM((rows, window), F32),
+                pltpu.VMEM((width, feats), BF16),
+                pltpu.VMEM((width, feats), BF16),
+                pltpu.VMEM((heads, rows, 2 * rows), F32),
+                pltpu.VMEM((heads, rows, width), F32),
+                pltpu.VMEM((heads, rows, width), F32),
                 pltpu.VMEM((window, width), F32),
                 pltpu.VMEM((window, width), F32),
                 pltpu.VMEM((REACH * rows, width), BF16),

time: 37.1 us -> 35.7 us (0.962)
  Pallas kernels: 35.4 us -> 34.2 us
    pallas_call x1, Pallas kernels: 34.2 us -> 33 us  [per_device(): pl.pallas_call(functools.partial(kernel, n_sec, n_ctx, rows, width, heads...]
where the time goes in v3:
time: 35.7 us; the launch traced here: 35.5 us
  Pallas kernels  34.2 us (96%)
  between operations  1.29 us (4%)
    pallas_call x1, Pallas kernels, per_device(): pl.pallas_call(functools.partial(kernel, n_sec, n_ctx, rows, width, heads...  33 us
    pallas_call x1, Pallas kernels, per_device(): pl.pallas_call(place, out_shape=shapes, in_specs=[anyw] * 5, out_specs=[h...  1.19 us

profile of v3, /device:TPU:16, one launch (start us, length us, event | category | flops | bytes accessed | tf_op | source)
XLA Modules:
  0.0 35.5 jit_solution(11021601443393636947)
XLA Ops:
  1.3 33.0 %attention.1 = (bf16[128,3072]{1,0:T(8,128)(2,1)S(1)}, bf16[128,3072]{1,0:T(8,128)(2,1)S(1)}, bf16[128,128]{1,0:T(8,128)(2,1)S(1)}, bf16[128,128]{1,0:T(8,128)(2,1)S(1)}, f32[16,128]{1,0:T(8,128)S(1)}) custom-call(bf16[128,3072]{1,0:T(8,128)(2,1)} %bitcast.9, bf16[128,128]{1,0:T(8,128)(2,1)} %bitcast.13, bf16[128,128]{1,0:T(8,128)(2,1)} %bitcast.14, ...), custom_call_target="tpu_custom_call" | custom-call | flops 3019898880 | bytes 3145728 | tf_op jit(solution)/shard_map/attention/pallas_call | solution.py:348
  34.3 1.2 %place.1 = (bf16[128,3072]{1,0:T(8,128)(2,1)}, bf16[128,3072]{1,0:T(8,128)(2,1)}, bf16[128,128]{1,0:T(8,128)(2,1)}, bf16[128,128]{1,0:T(8,128)(2,1)}, f32[16,128]{1,0:T(8,128)}) custom-call(bf16[128,3072]{1,0:T(8,128)(2,1)S(1)} %get-tuple-element.15.refs_0_, bf16[128,3072]{1,0:T(8,128)(2,1)S(1)} %get-tuple-element.16.refs_1_, ...), custom_call_target="tpu_custom_call" | custom-call | tf_op jit(solution)/shard_map/place/pallas_call | solution.py:403

commit v4 on v3

--- a/solution.py
+++ b/solution.py
@@ -178,6 +178,9 @@
     for c in fs:
         c.start()
     for h in range(heads):
+        if h == heads // 2:
+            pl.when(back4)(k2.wait_recv)
+            pl.when(odd == 1)(k4.start)
         qh = q[:, head(h)]
         s4 = dot(qh, kwin[block(4), :], NT) + bias[:, block(4)]
         s2 = dot(qh, kwin[block(2), :], NT) + bias[:, block(2)]
@@ -188,14 +191,6 @@
         early[h, :, rows:] = e4
         early_top[h] = jnp.broadcast_to(top, (rows, width))
         early_sum[h] = jnp.broadcast_to(jnp.sum(e4 + e2, axis=1, keepdims=True), (rows, width))
-
-    @pl.when(back4)
-    def _():
-        k2.wait_recv()
-
-    @pl.when(odd == 1)
-    def _():
-        k4.start()
 
     k3.wait_recv()
     k4.wait_recv()
@@ -237,6 +232,11 @@
         if lo == 0:
             vhome[block(1), :] = vparts[block(1), :].astype(BF16)
             dv4.start()
+
+            @pl.when(odd == 0)
+            def _():
+                vhome[block(0), :] = vparts[block(0), :].astype(BF16)
+                pl.when(back4)(dv2.start)
         if lo == 2:
             vhome[block(3), :] = vparts[block(3), :].astype(BF16)
             dv3.start()
@@ -249,9 +249,14 @@
             dv3.wait_recv()
             vparts[far, :] = vparts[far, :] + vpair[1].astype(F32)
             vparts[near, :] = vparts[near, :] + vpair[0].astype(F32)
-            vhome[block(0), :] = vparts[block(0), :].astype(BF16)
+
+            @pl.when(odd == 1)
+            def _():
+                vhome[block(0), :] = vparts[block(0), :].astype(BF16)
+                pl.when(back4)(dv2.start)
+
             vhome[block(2), :] = vparts[block(2), :].astype(BF16)
-            near_far(back2, back4, (dv1.start, dv2.start))
+            pl.when(back2)(dv1.start)
             for b in range(3):
                 term = (first_coef * vparts[block(mine[b]), :]).astype(BF16)
                 for s in range(n_sec):
@@ -275,14 +280,24 @@
     key_terms(0, 2)
     khome[block(1), :] = kparts[block(1), :].astype(BF16)
     dk4.start()
+
+    @pl.when(odd == 0)
+    def _():
+        khome[block(0), :] = kparts[block(0), :].astype(BF16)
+        pl.when(back4)(dk2.start)
+
     key_terms(2, 4)
     khome[block(3), :] = kparts[block(3), :].astype(BF16)
     dk3.start()
     key_terms(4, 5)
     dk4.wait_recv()
     kparts[far, :] = kparts[far, :] + kpair[1].astype(F32)
-    khome[block(0), :] = kparts[block(0), :].astype(BF16)
-    pl.when(back4)(dk2.start)
+
+    @pl.when(odd == 1)
+    def _():
+        khome[block(0), :] = kparts[block(0), :].astype(BF16)
+        pl.when(back4)(dk2.start)
+
     dk3.wait_recv()
     kparts[near, :] = kparts[near, :] + kpair[0].astype(F32)
     khome[block(2), :] = kparts[block(2), :].astype(BF16)

time: 35.7 us -> 35.2 us (0.986)
  Pallas kernels: 34.2 us -> 33.6 us
    pallas_call x1, Pallas kernels: 33 us -> 32.4 us  [per_device(): pl.pallas_call(functools.partial(kernel, n_sec, n_ctx, rows, width, heads...]
where the time goes in v4:
time: 35.2 us; the launch traced here: 34.8 us
  Pallas kernels  33.6 us (95%)
  between operations  1.29 us (4%)
    pallas_call x1, Pallas kernels, per_device(): pl.pallas_call(functools.partial(kernel, n_sec, n_ctx, rows, width, heads...  32.4 us
    pallas_call x1, Pallas kernels, per_device(): pl.pallas_call(place, out_shape=shapes, in_specs=[anyw] * 5, out_specs=[h...  1.19 us

profile of v4, /device:TPU:16, one launch (start us, length us, event | category | flops | bytes accessed | tf_op | source)
XLA Modules:
  0.0 34.8 jit_solution(14691379051775662272)
XLA Ops:
  1.3 32.4 %attention.1 = (bf16[128,3072]{1,0:T(8,128)(2,1)S(1)}, bf16[128,3072]{1,0:T(8,128)(2,1)S(1)}, bf16[128,128]{1,0:T(8,128)(2,1)S(1)}, bf16[128,128]{1,0:T(8,128)(2,1)S(1)}, f32[16,128]{1,0:T(8,128)S(1)}) custom-call(bf16[128,3072]{1,0:T(8,128)(2,1)} %bitcast.9, bf16[128,128]{1,0:T(8,128)(2,1)} %bitcast.13, bf16[128,128]{1,0:T(8,128)(2,1)} %bitcast.14, ...), custom_call_target="tpu_custom_call" | custom-call | flops 3019898880 | bytes 3145728 | tf_op jit(solution)/shard_map/attention/pallas_call | solution.py:363
  33.6 1.2 %place.1 = (bf16[128,3072]{1,0:T(8,128)(2,1)}, bf16[128,3072]{1,0:T(8,128)(2,1)}, bf16[128,128]{1,0:T(8,128)(2,1)}, bf16[128,128]{1,0:T(8,128)(2,1)}, f32[16,128]{1,0:T(8,128)}) custom-call(bf16[128,3072]{1,0:T(8,128)(2,1)S(1)} %get-tuple-element.15.refs_0_, bf16[128,3072]{1,0:T(8,128)(2,1)S(1)} %get-tuple-element.16.refs_1_, ...), custom_call_target="tpu_custom_call" | custom-call | tf_op jit(solution)/shard_map/place/pallas_call | solution.py:418
